TPU v7x, 32 devices: a whole 2x2x4 slice. The times are simulated.
32 devices in a mesh: node: 8 (over y, x, core), local: 4 (over z).
Axes of the slice: x: 2, y: 2, z: 4, core: 2. Of those that a mesh axis runs over, the one named last changes fastest.
Arguments:
- moe_in: bfloat16 [512, 3584], P(('node', 'local')), may hold values from -6 to 6
- route_ids: int32 [512, 8], P(('node', 'local')), may hold values from 0 to 31, as said below
- route_weights: float32 [512, 8], P(('node', 'local')), may hold values from 0.05 to 0.6
- w_gate: bfloat16 [32, 3584, 1024], P(('node', 'local')), may hold values from -0.09375 to 0.09375
- w_up: bfloat16 [32, 3584, 1024], P(('node', 'local')), may hold values from -0.09375 to 0.09375
- w_down: bfloat16 [32, 1024, 3584], P(('node', 'local')), may hold values from -0.1875 to 0.1875
- queries: bfloat16 [32, 128, 576], P(('node', 'local')), may hold values from -70 to 70
- cache_latent: bfloat16 [32, 2048, 512], P(('node', 'local')), may hold values from -12 to 12
- cache_rope: bfloat16 [32, 64, 2048], P(('node', 'local')), may hold values from -2 to 2
- lengths: int32 [32], P(('node', 'local')), may hold values from 256 to 2048, as said below
Outputs:
- moe_out: bfloat16 [512, 3584], P(('node', 'local'))
- attn_out: bfloat16 [32, 128, 512], P(('node', 'local'))
Inputs may be any that keep to these rules, and one draw needn't show every extreme that they name: `route_ids`: each row names 8 different experts, 2 in each of 4 different node groups; expert e lies in node group e // 4 and is held by the device of flat index e (node major). Within the rows of one device (aligned blocks of 16 rows) no node group is used by more than 16 rows and no expert is named by more than 8 rows; in every such block some node group is used by exactly 16 rows and each of its experts is named by exactly 8 rows. `lengths`: at least one row has all 2048 slots filled.
All inputs are finite; a program needn't handle non-finite values.
Results may differ from a plain program's by a relative error of at most 0.012.
Values may be sent and summed in bfloat16 or wider, within the bound.
A program may use at most 128 MiB of HBM per device.

v0:
```python
import jax
import jax.numpy as jnp
from jax import lax
from jax.sharding import PartitionSpec as P

score_scale = 192.0 ** (-0.5)


def expert_block(block, gate_one, up_one, down_one):
    model_width = block.shape[-1]
    rows_flat = block.reshape(-1, model_width)
    gate_act = jnp.dot(rows_flat, gate_one, preferred_element_type=jnp.float32)
    up_act = jnp.dot(rows_flat, up_one, preferred_element_type=jnp.float32)
    hidden_act = (jax.nn.silu(gate_act) * up_act).astype(jnp.bfloat16)
    result = jnp.dot(hidden_act, down_one, preferred_element_type=jnp.float32).astype(jnp.bfloat16)
    return result.reshape(block.shape)


def attention(queries, cache_latent, cache_rope, lengths):
    kv_width = cache_latent.shape[-1]
    scores = jnp.einsum(
        "rhc,rkc->rhk", queries[:, :, :kv_width], cache_latent, preferred_element_type=jnp.float32
    )
    scores = (
        scores
        + jnp.einsum(
            "rhc,rck->rhk", queries[:, :, kv_width:], cache_rope, preferred_element_type=jnp.float32
        )
    ) * score_scale
    positions = jnp.arange(cache_latent.shape[1], dtype=jnp.int32)
    scores = jnp.where(positions[None, None, :] < lengths[:, None, None], scores, -jnp.inf)
    peak = jnp.max(scores, axis=-1, keepdims=True)
    weights = jnp.exp(scores - peak)
    probs = (weights / jnp.sum(weights, axis=-1, keepdims=True)).astype(jnp.bfloat16)
    return jnp.einsum(
        "rhk,rkc->rhc", probs, cache_latent, preferred_element_type=jnp.float32
    ).astype(jnp.bfloat16)


def local(
    moe_in,
    route_ids,
    route_weights,
    w_gate,
    w_up,
    w_down,
    queries,
    cache_latent,
    cache_rope,
    lengths,
):
    attn_out = attention(queries, cache_latent, cache_rope, lengths)
    node_count = lax.axis_size("node")
    local_count = lax.axis_size("local")
    expert_count = node_count * local_count
    row_count, model_width = moe_in.shape
    top_count = route_ids.shape[1]
    capacity = 2 * row_count * top_count // expert_count
    gate_one = w_gate[0]
    up_one = w_up[0]
    down_one = w_down[0]
    row_index = jnp.broadcast_to(jnp.arange(row_count, dtype=jnp.int32)[:, None], route_ids.shape)
    padded = jnp.concatenate([moe_in, jnp.zeros((1, model_width), moe_in.dtype)], axis=0)
    expert_hits = (
        route_ids[:, :, None] == jnp.arange(expert_count, dtype=jnp.int32)[None, None, :]
    ).astype(jnp.int32)
    present = jnp.sum(expert_hits, axis=1, dtype=jnp.int32)
    earlier = jnp.cumsum(present, axis=0, dtype=jnp.int32) - present
    rank_of = jnp.sum(expert_hits * earlier[:, None, :], axis=-1, dtype=jnp.int32)
    slot_of = route_ids * capacity + rank_of
    table = (
        jnp.full((expert_count * capacity,), row_count, jnp.int32)
        .at[slot_of.reshape(-1)]
        .set(row_index.reshape(-1))
    )
    outgoing = padded[table].reshape(expert_count, capacity, model_width)
    result = expert_block(
        lax.all_to_all(outgoing, ("node", "local"), split_axis=0, concat_axis=0, tiled=True),
        gate_one,
        up_one,
        down_one,
    )
    returned = lax.all_to_all(result, ("node", "local"), split_axis=0, concat_axis=0, tiled=True)
    picked = returned.reshape(expert_count * capacity, model_width)[slot_of]
    total = jnp.einsum("rk,rkd->rd", route_weights, picked.astype(jnp.float32))
    moe_out = total.astype(jnp.bfloat16)
    return (moe_out, attn_out)


def solution(mesh):
    placed = (
        P(("node", "local"), None),
        P(("node", "local"), None),
        P(("node", "local"), None),
        P(("node", "local"), None, None),
        P(("node", "local"), None, None),
        P(("node", "local"), None, None),
        P(("node", "local"), None, None),
        P(("node", "local"), None, None),
        P(("node", "local"), None, None),
        P(("node", "local")),
    )
    return jax.shard_map(
        local,
        mesh=mesh,
        in_specs=placed,
        out_specs=(P(("node", "local"), None), P(("node", "local"), None, None)),
        check_vma=False,
    )
```

profile of v0, /device:TPU:0, one launch (start us, length us, event | category | flops | bytes accessed | tf_op | source)
XLA Modules:
  0.0 124.8 jit_solution(12187405727765045536)
XLA Ops:
  0.6 0.0 copy-start
  0.6 0.9 copy.18
  1.6 0.1 convert_reduce_fusion
  1.7 0.4 select_reduce_fusion
  2.1 0.1 reshape.106
  2.2 0.1 reshape.136
  2.3 1.0 scatter_custom_fusion
  3.3 0.9 concatenate.3
  4.3 3.0 %gather_fusion = bf16[256,3584]{1,0:T(8,128)(2,1)} fusion(bf16[17,3584]{1,0:T(8,128)(2,1)S(1)} %concatenate.3, s32[1024]{0:T(1024)S(1)} %pad_clamp_fusion.1), kind=kCustom, calls=%fused_computation | custom fusion | bytes 3671040 | tf_op jit(solution)/shard_map/gather | solution.py:76
  7.2 49.4 %all_to_all.10 = bf16[32,8,3584]{2,1,0:T(8,128)(2,1)S(1)} all-to-all(bf16[32,8,3584]{2,1,0:T(8,128)(2,1)} %bitcast.70), channel_id=1, replica_groups=mesh['node'=8,'local'=4] {'node','local'}, dimensions={0} | all-to-all | bytes 3670016 | tf_op jit(solution)/shard_map/all_to_all | solution.py:78
  56.6 1.2 copy-done.1
  57.9 5.1 %fusion.4 = f32[256,1024]{1,0:T(8,128)S(1)} fusion(bf16[1,3584,1024]{2,1,0:T(8,128)(2,1)} %param.13, bf16[32,8,3584]{2,1,0:T(8,128)(2,1)S(1)} %all_to_all.10), kind=kOutput, calls=%fused_computation.7 | convolution fusion | flops 1879048192 | bytes 10223616 | tf_op jit(solution)/shard_map/dot_general | solution.py:12
  63.0 11.0 %fusion.9 = bf16[32,8,3584]{2,1,0:T(8,128)(2,1)} fusion(bf16[1,1024,3584]{2,1,0:T(8,128)(2,1)} %param.15, bf16[1,3584,1024]{2,1,0:T(8,128)(2,1)} %param.14, bf16[32,8,3584]{2,1,0:T(8,128)(2,1)} %copy-done.1, f32[256,1024]{1,0:T(8,128)S(1)} %fusion.4), kind=kOutput, calls=%fused_computation.10 | convolution fusion | flops 3760586752 | bytes 19398656 | tf_op jit(solution)/shard_map/dot_general | solution.py:15
  74.0 4.5 %all-to-all-start.1 = ((bf16[32,8,3584]{2,1,0:T(8,128)(2,1)}), bf16[32,8,3584]{2,1,0:T(8,128)(2,1)}, u32[]{:S(2)}, u32[]{:S(2)}) async-start(bf16[32,8,3584]{2,1,0:T(8,128)(2,1)} %fusion.9), calls=%async_computation.1 | async-start | bytes 3670016 | tf_op jit(solution)/shard_map/all_to_all | solution.py:83
  78.5 0.1 reshape.126
  78.6 0.1 copy.20
  79.4 0.8 fusion.16
  80.2 0.4 fusion.55
  80.6 0.3 fusion.36
  80.9 1.2 fusion.33
  82.1 37.8 %all-to-all-done.1 = bf16[32,8,3584]{2,1,0:T(8,128)(2,1)} async-done(((bf16[32,8,3584]{2,1,0:T(8,128)(2,1)}), bf16[32,8,3584]{2,1,0:T(8,128)(2,1)}, u32[]{:S(2)}, u32[]{:S(2)}) %all-to-all-start.1) | async-done | bytes 1835040 | tf_op jit(solution)/shard_map/all_to_all | solution.py:83
  120.0 3.8 %gather_fusion.1 = bf16[128,3584]{1,0:T(8,128)(2,1)S(1)} fusion(bf16[256,3584]{1,0:T(8,128)(2,1)} %bitcast.7, s32[1024]{0:T(1024)S(1)} %pad_clamp_fusion), kind=kCustom, calls=%fused_computation.1 | custom fusion | bytes 1835520 | tf_op jit(solution)/shard_map/gather | solution.py:84
  123.7 0.4 fusion.37
  124.1 0.7 copy.23
  (17 shorter events, 0.1 us)
Async XLA Ops:
  0.6 78.8 %copy-start = (bf16[1,2048,512]{2,1,0:T(8,128)(2,1)S(1)}, bf16[1,2048,512]{2,1,0:T(8,128)(2,1)}, u32[]{:S(2)}) copy-start(bf16[1,2048,512]{2,1,0:T(8,128)(2,1)} %param.17) | copy-start | bytes 6291460
  56.6 1.2 copy-start.1
  74.0 4.6 %copy-start.4 = (f32[16,8]{0,1:T(8,128)S(1)}, f32[16,8]{0,1:T(8,128)}, u32[]{:S(2)}) copy-start(f32[16,8]{0,1:T(8,128)} %param.12) | copy-start | bytes 1540
  74.0 5.4 %copy-start.3 = (bf16[1,128,576]{1,2,0:T(8,128)(2,1)S(1)}, bf16[1,128,576]{1,2,0:T(8,128)(2,1)}, u32[]{:S(2)}) copy-start(bf16[1,128,576]{1,2,0:T(8,128)(2,1)} %param.16) | copy-start | bytes 442372
  74.0 45.9 %all-to-all-start.1 = ((bf16[32,8,3584]{2,1,0:T(8,128)(2,1)}), bf16[32,8,3584]{2,1,0:T(8,128)(2,1)}, u32[]{:S(2)}, u32[]{:S(2)}) async-start(bf16[32,8,3584]{2,1,0:T(8,128)(2,1)} %fusion.9), calls=%async_computation.1 | async-start | bytes 3670016 | tf_op jit(solution)/shard_map/all_to_all | solution.py:83
  78.5 1.7 %copy-start.2 = (bf16[1,64,2048]{2,1,0:T(8,128)(2,1)S(1)}, bf16[1,64,2048]{2,1,0:T(8,128)(2,1)}, u32[]{:S(2)}) copy-start(bf16[1,64,2048]{2,1,0:T(8,128)(2,1)} %param.18) | copy-start | bytes 786436
where the time goes:
time: 126 us; the launch traced here: 125 us
  blocking collectives  49.4 us (39%)
  waiting for transfers between devices  37.8 us (30%)
  matrix products  18.9 us (15%)
  local copies, waits for them, and re-layouts  11.8 us (9%)
  starting transfers between devices  4.48 us (4%)
  between operations  1.46 us (1%)
    all_to_all x1, blocking collectives, local(): lax.all_to_all(outgoing, ('node', 'local'), split_axis=0, concat_axis=0,...  49.4 us
    all_to_all x1, waiting for transfers between devices, local(): lax.all_to_all(result, ('node', 'local'), split_axis=0, concat_axis=0, ti...  37.8 us
    dot_general x1, matrix products, expert_block(): jnp.dot(hidden_act, down_one, preferred_element_type=jnp.float32)  11 us
    dot_general x1, matrix products, expert_block(): gate_act = jnp.dot(rows_flat, gate_one, preferred_element_type=jnp.float32)  5.13 us
    all_to_all x1, starting transfers between devices, local(): lax.all_to_all(result, ('node', 'local'), split_axis=0, concat_axis=0, ti...  4.48 us
    gather x1, local copies, waits for them, and re-layouts, local(): picked = returned.reshape(expert_count * capacity, model_width)[slot_of]  3.76 us
    gather x1, local copies, waits for them, and re-layouts, local(): outgoing = padded[table].reshape(expert_count, capacity, model_width)  2.98 us
  transfers between devices with their start and end apart: 1, of which 1 were waited for; matrix products, arithmetic and copies ran while one was open for 2% of the time, Pallas kernels for 0%

commit v1 on v0

--- a/solution.py
+++ b/solution.py
@@ -1,9 +1,16 @@
+import functools
+
 import jax
 import jax.numpy as jnp
 from jax import lax
+from jax.experimental import pallas as pl
+from jax.experimental.pallas import tpu as pltpu
 from jax.sharding import PartitionSpec as P
 
 score_scale = 192.0 ** (-0.5)
+MESH = pl.DeviceIdType.MESH
+ROUTE_LANES = 128
+ATT_PIECES = 4
 
 
 def expert_block(block, gate_one, up_one, down_one):
@@ -37,7 +44,7 @@
     ).astype(jnp.bfloat16)
 
 
-def local(
+def local_general(
     moe_in,
     route_ids,
     route_weights,
@@ -50,15 +57,10 @@
     lengths,
 ):
     attn_out = attention(queries, cache_latent, cache_rope, lengths)
-    node_count = lax.axis_size("node")
-    local_count = lax.axis_size("local")
-    expert_count = node_count * local_count
+    expert_count = lax.axis_size("node") * lax.axis_size("local")
     row_count, model_width = moe_in.shape
     top_count = route_ids.shape[1]
     capacity = 2 * row_count * top_count // expert_count
-    gate_one = w_gate[0]
-    up_one = w_up[0]
-    down_one = w_down[0]
     row_index = jnp.broadcast_to(jnp.arange(row_count, dtype=jnp.int32)[:, None], route_ids.shape)
     padded = jnp.concatenate([moe_in, jnp.zeros((1, model_width), moe_in.dtype)], axis=0)
     expert_hits = (
@@ -76,15 +78,457 @@
     outgoing = padded[table].reshape(expert_count, capacity, model_width)
     result = expert_block(
         lax.all_to_all(outgoing, ("node", "local"), split_axis=0, concat_axis=0, tiled=True),
-        gate_one,
-        up_one,
-        down_one,
+        w_gate[0],
+        w_up[0],
+        w_down[0],
     )
     returned = lax.all_to_all(result, ("node", "local"), split_axis=0, concat_axis=0, tiled=True)
     picked = returned.reshape(expert_count * capacity, model_width)[slot_of]
     total = jnp.einsum("rk,rkd->rd", route_weights, picked.astype(jnp.float32))
-    moe_out = total.astype(jnp.bfloat16)
-    return (moe_out, attn_out)
+    return (total.astype(jnp.bfloat16), attn_out)
+
+
+def fused_kernel(
+    dims,
+    capacity,
+    x_ref,
+    ids_ref,
+    rw_ref,
+    len_ref,
+    q_ref,
+    gate_hbm,
+    up_hbm,
+    down_hbm,
+    latent_hbm,
+    rope_hbm,
+    moe_ref,
+    attn_ref,
+    gathered,
+    part,
+    recv_core,
+    sum_core,
+    recv_one,
+    sum_one,
+    recv_two,
+    sum_two,
+    recv_z,
+    gate_w,
+    up_w,
+    down_w,
+    latent,
+    rope,
+    scores,
+    attn_acc,
+    gate_acc,
+    up_acc,
+    pick,
+    spread,
+    load_sem,
+    cache_sem,
+    ag_send,
+    ag_recv,
+    rs_send,
+    rs_recv,
+):
+    ny, nx, nc, nz = dims
+    rows, width = x_ref.shape
+    chunks = len(gathered)
+    cw = width // chunks
+    tokens = ny * nx * nc * nz * rows
+    slots_total = ny * nx * nc * nz * capacity
+    hidden = gate_w.shape[1]
+    f32, bf16 = jnp.float32, jnp.bfloat16
+
+    node = lax.axis_index("node")
+    z = lax.axis_index("local")
+    core = lax.rem(node, nc)
+    x = lax.rem(node // nc, nx)
+    y = node // (nc * nx)
+    me = node * nz + z
+
+    def device(yy, xx, cc, zz):
+        return ((yy * nx + xx) * nc + cc, zz)
+
+    core_dev = device(y, x, 1 - core, z)
+    x_dev = device(y, 1 - x, core, z)
+    y_dev = device(1 - y, x, core, z)
+    z_at = [lax.rem(z + o, nz) for o in range(nz)]
+    z_devs = [device(y, x, core, z_at[o]) for o in range(1, nz)]
+
+    barrier = pltpu.get_barrier_semaphore()
+    for dev in [core_dev, x_dev, y_dev] + z_devs:
+        pl.semaphore_signal(barrier, inc=1, device_id=dev, device_id_type=MESH)
+
+    cache_loads = [
+        pltpu.make_async_copy(latent_hbm.at[0], latent, cache_sem.at[0]),
+        pltpu.make_async_copy(rope_hbm.at[0], rope, cache_sem.at[1]),
+    ]
+    for load in cache_loads:
+        load.start()
+    gate_loads, up_loads, down_loads = [], [], []
+    for c in range(chunks):
+        at = pl.ds(c * cw, cw)
+        gate_loads.append(
+            pltpu.make_async_copy(gate_hbm.at[0, at], gate_w.at[at], load_sem.at[0, c])
+        )
+        up_loads.append(pltpu.make_async_copy(up_hbm.at[0, at], up_w.at[at], load_sem.at[1, c]))
+        down_loads.append(
+            pltpu.make_async_copy(down_hbm.at[0, :, at], down_w.at[c], load_sem.at[2, c])
+        )
+    for c in range(chunks):
+        gate_loads[c].start()
+        up_loads[c].start()
+    for c in range(chunks):
+        down_loads[c].start()
+
+    lanes = lax.broadcasted_iota(jnp.int32, (rows, ROUTE_LANES), 1)
+    ids = jnp.transpose(ids_ref[...])
+    rw = jnp.transpose(rw_ref[...])
+    table = jnp.zeros((rows, ROUTE_LANES), f32)
+    for k in range(ids.shape[1]):
+        table = table + jnp.where(lanes == ids[:, k : k + 1], rw[:, k : k + 1], 0.0)
+    gathered[0][y, x, core, z, :, :ROUTE_LANES] = table.astype(bf16)
+    gathered[0][y, x, core, z, :, ROUTE_LANES:] = x_ref[:, :cw]
+    for c in range(1, chunks):
+        gathered[c][y, x, core, z] = x_ref[:, c * cw : (c + 1) * cw]
+
+    pl.semaphore_wait(barrier, 2 + nz)
+
+    sends = []
+
+    def push(src, dst, send_sem, recv_sem, dev):
+        copy = pltpu.make_async_remote_copy(
+            src_ref=src,
+            dst_ref=dst,
+            send_sem=send_sem,
+            recv_sem=recv_sem,
+            device_id=dev,
+            device_id_type=MESH,
+        )
+        copy.start()
+        sends.append(copy)
+
+    def arrived(dst, send_sem, recv_sem, dev):
+        pltpu.make_async_remote_copy(
+            src_ref=dst,
+            dst_ref=dst,
+            send_sem=send_sem,
+            recv_sem=recv_sem,
+            device_id=dev,
+            device_id_type=MESH,
+        ).wait_recv()
+
+    def gather_z(c):
+        own = gathered[c].at[y, x, core, z]
+        for o in range(1, nz):
+            push(own, own, ag_send.at[c, o - 1], ag_recv.at[c, o - 1], z_devs[o - 1])
+
+    def gather_z_wait(c):
+        for o in range(1, nz):
+            arrived(
+                gathered[c].at[y, x, core, z_at[nz - o]],
+                ag_send.at[c, o - 1],
+                ag_recv.at[c, o - 1],
+                z_devs[nz - o - 1],
+            )
+
+    def gather_views(c):
+        first = gathered[c].at[y, x, core]
+        if c % 2 == 0:
+            return [
+                (first, gathered[c].at[y, 1 - x, core], x_dev),
+                (gathered[c].at[y, :, core], gathered[c].at[1 - y, :, core], y_dev),
+                (gathered[c].at[:, :, core], gathered[c].at[:, :, 1 - core], core_dev),
+            ]
+        return [
+            (first, gathered[c].at[1 - y, x, core], y_dev),
+            (gathered[c].at[:, x, core], gathered[c].at[:, 1 - x, core], x_dev),
+            (gathered[c].at[:, :, core], gathered[c].at[:, :, 1 - core], core_dev),
+        ]
+
+    def gather_push(c, phase):
+        src, _, dev = gather_views(c)[phase]
+        k = nz - 1 + phase
+        push(src, src, ag_send.at[c, k], ag_recv.at[c, k], dev)
+
+    def gather_wait(c, phase):
+        _, dst, dev = gather_views(c)[phase]
+        k = nz - 1 + phase
+        arrived(dst, ag_send.at[c, k], ag_recv.at[c, k], dev)
+
+    kv = latent.shape[1]
+    cache = latent.shape[0]
+    piece = cache // ATT_PIECES
+    length = len_ref[0]
+
+    def score_piece(i):
+        at = slice(i * piece, (i + 1) * piece)
+        s = jnp.dot(latent[at, :], q_ref[0, :kv, :], preferred_element_type=f32)
+        s = s + lax.dot_general(
+            rope[:, at], q_ref[0, kv:, :], (((0,), (0,)), ((), ())), preferred_element_type=f32
+        )
+        positions = lax.broadcasted_iota(jnp.int32, s.shape, 0) + i * piece
+        scores[at, :] = jnp.where(positions < length, s * score_scale, -jnp.inf)
+
+    def soft():
+        s = scores[...]
+        e = jnp.exp(s - jnp.max(s, axis=0, keepdims=True))
+        scores[...] = e / jnp.sum(e, axis=0, keepdims=True)
+
+    def value_piece(i):
+        at = slice(i * piece, (i + 1) * piece)
+        got = lax.dot_general(
+            scores[at, :].astype(bf16),
+            latent[at, :],
+            (((0,), (0,)), ((), ())),
+            preferred_element_type=f32,
+        )
+        if i == 0:
+            attn_acc[...] = got
+        elif i < ATT_PIECES - 1:
+            attn_acc[...] += got
+        else:
+            attn_ref[0] = (attn_acc[...] + got).astype(bf16)
+
+    def first_piece():
+        for load in cache_loads:
+            load.wait()
+        score_piece(0)
+
+    tasks = [first_piece]
+    tasks += [functools.partial(score_piece, i) for i in range(1, ATT_PIECES)]
+    tasks += [soft]
+    tasks += [functools.partial(value_piece, i) for i in range(ATT_PIECES)]
+
+    def route():
+        sent = gathered[0][:, :, :, :, :, :ROUTE_LANES].reshape(tokens, ROUTE_LANES)
+        mine = (lax.broadcasted_iota(jnp.int32, (16, ROUTE_LANES), 1) == me).astype(bf16)
+        weight = lax.dot_general(
+            mine, sent, (((1,), (1,)), ((), ())), preferred_element_type=f32
+        )
+        present = weight > 0.0
+        t_from = lax.broadcasted_iota(jnp.int32, (tokens, tokens), 0)
+        t_to = lax.broadcasted_iota(jnp.int32, (tokens, tokens), 1)
+        before = ((t_from < t_to) & (t_from // rows == t_to // rows)).astype(bf16)
+        rank = jnp.dot(present.astype(bf16), before, preferred_element_type=f32)
+        base = (lax.broadcasted_iota(jnp.int32, (16, tokens), 1) // rows) * capacity
+        slot = jnp.where(present, rank + base.astype(f32), -1.0)
+        slot_id = lax.broadcasted_iota(jnp.int32, (slots_total, tokens), 0).astype(f32)
+        hit = slot[0:1, :] == slot_id
+        pick[...] = hit.astype(bf16)
+        spread[...] = jnp.transpose(jnp.where(hit, weight[0:1, :], 0.0)).astype(bf16)
+
+    def expert_in(c):
+        g = gathered[c][...] if c else gathered[c][:, :, :, :, :, ROUTE_LANES:]
+        rows_in = jnp.dot(
+            pick[...], g.reshape(tokens, cw), preferred_element_type=f32
+        ).astype(bf16)
+        gate_loads[c].wait()
+        up_loads[c].wait()
+        at = slice(c * cw, (c + 1) * cw)
+        for acc, w in ((gate_acc, gate_w), (up_acc, up_w)):
+            got = jnp.dot(rows_in, w[at, :], preferred_element_type=f32)
+            if c == 0:
+                acc[...] = got
+            else:
+                acc[...] += got
+
+    for c in range(chunks):
+        gather_z(c)
+    for s in range(chunks + 3):
+        if s < chunks:
+            gather_z_wait(s)
+            gather_push(s, 0)
+        for phase in range(2):
+            c = s - 1 - phase
+            if 0 <= c < chunks:
+                gather_wait(c, phase)
+                gather_push(c, phase + 1)
+        if tasks:
+            tasks.pop(0)()
+        c = s - 3
+        if 0 <= c < chunks:
+            gather_wait(c, 2)
+            if c == 0:
+                route()
+            expert_in(c)
+    for task in tasks:
+        task()
+
+    gate = gate_acc[...]
+    hidden_act = (gate / (1.0 + jnp.exp(-gate)) * up_acc[...]).astype(bf16)
+
+    def add_to(dst, a, b):
+        dst[...] = (a.astype(f32) + b.astype(f32)).astype(bf16)
+
+    def out_views(c):
+        if c % 2 == 0:
+            return [
+                (part[c].at[:, :, 1 - core], recv_core[c], core_dev),
+                (sum_core[c].at[1 - y], recv_one[c], y_dev),
+                (sum_one[c].at[1 - x], recv_two[c], x_dev),
+            ]
+        return [
+            (part[c].at[:, :, 1 - core], recv_core[c], core_dev),
+            (sum_core[c].at[:, 1 - x], recv_one[c], x_dev),
+            (sum_one[c].at[1 - y], recv_two[c], y_dev),
+        ]
+
+    def out_push(c, phase):
+        src, dst, dev = out_views(c)[phase]
+        push(src, dst, rs_send.at[c, phase], rs_recv.at[c, phase], dev)
+
+    def out_wait(c, phase):
+        _, dst, dev = out_views(c)[phase]
+        arrived(dst, rs_send.at[c, phase], rs_recv.at[c, phase], dev)
+
+    def stage_zero(c):
+        down_loads[c].wait()
+        out = jnp.dot(hidden_act, down_w[c], preferred_element_type=f32).astype(bf16)
+        got = jnp.dot(spread[...], out, preferred_element_type=f32).astype(bf16)
+        part[c][...] = got.reshape(part[c].shape)
+        out_push(c, 0)
+
+    def stage_one(c):
+        out_wait(c, 0)
+        add_to(sum_core[c], part[c][:, :, core], recv_core[c][...])
+        out_push(c, 1)
+
+    def stage_two(c):
+        out_wait(c, 1)
+        kept = sum_core[c][y] if c % 2 == 0 else sum_core[c][:, x]
+        add_to(sum_one[c], kept, recv_one[c][...])
+        out_push(c, 2)
+
+    def stage_three(c):
+        out_wait(c, 2)
+        kept = sum_one[c][x] if c % 2 == 0 else sum_one[c][y]
+        add_to(sum_two[c], kept, recv_two[c][...])
+        for o in range(1, nz):
+            push(
+                sum_two[c].at[z_at[o]],
+                recv_z[c].at[o - 1],
+                rs_send.at[c, 2 + o],
+                rs_recv.at[c, 2 + o],
+                z_devs[o - 1],
+            )
+
+    def stage_four(c):
+        total = sum_two[c][z].astype(f32)
+        for o in range(1, nz):
+            arrived(
+                recv_z[c].at[o - 1], rs_send.at[c, 2 + o], rs_recv.at[c, 2 + o], z_devs[nz - o - 1]
+            )
+            total = total + recv_z[c][o - 1].astype(f32)
+        moe_ref[:, c * cw : (c + 1) * cw] = total.astype(bf16)
+
+    stages = [stage_zero, stage_one, stage_two, stage_three, stage_four]
+    for s in range(chunks + len(stages) - 1):
+        for k, stage in enumerate(stages):
+            c = s - k
+            if 0 <= c < chunks:
+                stage(c)
+
+    for copy in sends:
+        copy.wait_send()
+
+
+def local_fused(
+    dims,
+    moe_in,
+    route_ids,
+    route_weights,
+    w_gate,
+    w_up,
+    w_down,
+    queries,
+    cache_latent,
+    cache_rope,
+    lengths,
+):
+    ny, nx, nc, nz = dims
+    experts = ny * nx * nc * nz
+    rows, width = moe_in.shape
+    capacity = 2 * rows * route_ids.shape[1] // experts
+    hidden = w_gate.shape[2]
+    cache, kv = cache_latent.shape[1:]
+    heads = queries.shape[1]
+    tokens = experts * rows
+    chunks = 7
+    cw = width // chunks
+    bf16, f32 = jnp.bfloat16, jnp.float32
+
+    def each(shape, extra=0):
+        return [
+            pltpu.VMEM(shape + (cw + (extra if c == 0 else 0),), bf16) for c in range(chunks)
+        ]
+
+    vmem = pl.BlockSpec(memory_space=pltpu.VMEM)
+    hbm = pl.BlockSpec(memory_space=pl.ANY)
+    moe_out, attn_out = pl.pallas_call(
+        functools.partial(fused_kernel, dims, capacity),
+        out_shape=(
+            jax.ShapeDtypeStruct((rows, width), bf16),
+            jax.ShapeDtypeStruct((1, heads, kv), bf16),
+        ),
+        in_specs=[
+            vmem,
+            vmem,
+            vmem,
+            pl.BlockSpec(memory_space=pltpu.SMEM),
+            vmem,
+            hbm,
+            hbm,
+            hbm,
+            hbm,
+            hbm,
+        ],
+        out_specs=(vmem, vmem),
+        scratch_shapes=[
+            each((ny, nx, nc, nz, rows), ROUTE_LANES),
+            each((ny, nx, nc, nz, rows)),
+            each((ny, nx, nz, rows)),
+            each((ny, nx, nz, rows)),
+            each((2, nz, rows)),
+            each((2, nz, rows)),
+            each((nz, rows)),
+            each((nz, rows)),
+            each((nz - 1, rows)),
+            pltpu.VMEM((width, hidden), bf16),
+            pltpu.VMEM((width, hidden), bf16),
+            pltpu.VMEM((chunks, hidden, cw), bf16),
+            pltpu.VMEM((cache, kv), bf16),
+            pltpu.VMEM(cache_rope.shape[1:], bf16),
+            pltpu.VMEM((cache, heads), f32),
+            pltpu.VMEM((heads, kv), f32),
+            pltpu.VMEM((experts * capacity, hidden), f32),
+            pltpu.VMEM((experts * capacity, hidden), f32),
+            pltpu.VMEM((experts * capacity, tokens), bf16),
+            pltpu.VMEM((tokens, experts * capacity), bf16),
+            pltpu.SemaphoreType.DMA((3, chunks)),
+            pltpu.SemaphoreType.DMA((2,)),
+            pltpu.SemaphoreType.DMA((chunks, nz + 2)),
+            pltpu.SemaphoreType.DMA((chunks, nz + 2)),
+            pltpu.SemaphoreType.DMA((chunks, nz + 2)),
+            pltpu.SemaphoreType.DMA((chunks, nz + 2)),
+        ],
+        compiler_params=pltpu.CompilerParams(
+            collective_id=0, has_side_effects=True, vmem_limit_bytes=60 * 1024 * 1024
+        ),
+        name="fused_moe_attention",
+    )(
+        moe_in,
+        jnp.transpose(route_ids),
+        jnp.transpose(route_weights),
+        lengths,
+        jnp.transpose(queries, (0, 2, 1)),
+        w_gate,
+        w_up,
+        w_down,
+        cache_latent,
+        cache_rope,
+    )
+    return moe_out, attn_out
 
 
 def solution(mesh):
@@ -100,6 +544,10 @@
         P(("node", "local"), None, None),
         P(("node", "local")),
     )
+    if mesh.shape["node"] == 8 and mesh.shape["local"] == 4:
+        local = functools.partial(local_fused, (2, 2, 2, 4))
+    else:
+        local = local_general
     return jax.shard_map(
         local,
         mesh=mesh,

time: 126 us -> 79.9 us (0.63)
  Pallas kernels: 0 us -> 75.3 us
  blocking collectives: 49.4 us -> 0 us
  waiting for transfers between devices: 37.8 us -> 0 us
  matrix products: 18.9 us -> 0 us
  local copies, waits for them, and re-layouts: 11.8 us -> 3.12 us
  starting transfers between devices: 4.48 us -> 0 us
    pallas_call x0 -> x1, Pallas kernels: none -> 75.3 us  [local_fused(): pl.pallas_call(functools.partial(fused_kernel, dims, capacity), out_shape...]
    all_to_all x1 -> x0, blocking collectives: 49.4 us -> none  [local(): lax.all_to_all(outgoing, ('node', 'local'), split_axis=0, concat_axis=0,...]
    all_to_all x1 -> x0, waiting for transfers between devices: 37.8 us -> none  [local(): lax.all_to_all(result, ('node', 'local'), split_axis=0, concat_axis=0, ti...]
    dot_general x6 -> x0, matrix products: 18.9 us -> none  [the longest x1 11 us: expert_block(): jnp.dot(hidden_act, down_one, preferred_element_type=jnp.float32)]
    gather x2 -> x0, local copies, waits for them, and re-layouts: 6.74 us -> none  [the longest x1 3.76 us: local(): picked = returned.reshape(expert_count * capacity, model_width)[slot_of]]
    all_to_all x1 -> x0, starting transfers between devices: 4.48 us -> none  [local(): lax.all_to_all(result, ('node', 'local'), split_axis=0, concat_axis=0, ti...]
    unnamed x12 -> x2, local copies, waits for them, and re-layouts: 2.24 us -> 3.12 us
  transfers between devices with their start and end apart: 1 -> 0, of which waited for: 1 -> 0; matrix products, arithmetic and copies ran while one was open for 2% -> 0% of each run, Pallas kernels for 0% -> 0%
where the time goes in v1:
time: 79.9 us; the launch traced here: 79.7 us
  Pallas kernels  75.3 us (94%)
  local copies, waits for them, and re-layouts  3.12 us (4%)
  between operations  1.29 us (2%)
    pallas_call x1, Pallas kernels, local_fused(): pl.pallas_call(functools.partial(fused_kernel, dims, capacity), out_shape...  75.3 us
    unnamed x2, local copies, waits for them, and re-layouts  3.12 us

profile of v1, /device:TPU:0, one launch (start us, length us, event | category | flops | bytes accessed | tf_op | source)
XLA Modules:
  0.0 79.7 jit_solution(8474074367396630101)
XLA Ops:
  1.3 75.3 %fused_moe_attention.1 = (bf16[16,3584]{1,0:T(8,128)(2,1)}, bf16[1,128,512]{2,1,0:T(8,128)(2,1)}) custom-call(bf16[16,3584]{1,0:T(8,128)(2,1)} %x_ref.1, s32[8,16]{1,0:T(8,128)} %bitcast.4, f32[8,16]{1,0:T(8,128)} %bitcast.5, s32[1]{0:T(128)S(6)} %copy.14.len_ref, bf16[1,576,128]{2,1,0:T(8,128)(2,1)} %bitcast.3, bf16[1,3584,1024]{2,1,0:T(8,128)(2,1)} %gate_hbm.1, ...), custom_call_target="tpu_custom_call" | custom-call | tf_op jit(solution)/shard_map/fused_moe_attention/pallas_call | solution.py:468
  76.6 1.6 %copy.15 = bf16[16,3584]{1,0:T(8,128)(2,1)} copy(bf16[16,3584]{1,0:T(8,128)(2,1)} %get-tuple-element.4) | data formatting | bytes 229376
  78.1 1.6 %copy.16 = bf16[1,128,512]{2,1,0:T(8,128)(2,1)} copy(bf16[1,128,512]{2,1,0:T(8,128)(2,1)} %get-tuple-element.5) | data formatting | bytes 262144

commit v2 on v1

--- a/solution.py
+++ b/solution.py
@@ -11,6 +11,10 @@
 MESH = pl.DeviceIdType.MESH
 ROUTE_LANES = 128
 ATT_PIECES = 4
+IN_STEPS = 7
+OUT_LAGS = (0, 1, 3, 5, 7)
+CHUNKS = 7
+VMEM_BYTES = 60 * 1024 * 1024
 
 
 def expert_block(block, gate_one, up_one, down_one):
@@ -134,6 +138,7 @@
     rows, width = x_ref.shape
     chunks = len(gathered)
     cw = width // chunks
+    merge = chunks // IN_STEPS
     tokens = ny * nx * nc * nz * rows
     slots_total = ny * nx * nc * nz * capacity
     hidden = gate_w.shape[1]
@@ -166,18 +171,20 @@
     for load in cache_loads:
         load.start()
     gate_loads, up_loads, down_loads = [], [], []
+    for m in range(chunks // merge):
+        at = pl.ds(m * merge * cw, merge * cw)
+        gate_loads.append(
+            pltpu.make_async_copy(gate_hbm.at[0, at], gate_w.at[at], load_sem.at[0, m])
+        )
+        up_loads.append(pltpu.make_async_copy(up_hbm.at[0, at], up_w.at[at], load_sem.at[1, m]))
     for c in range(chunks):
         at = pl.ds(c * cw, cw)
-        gate_loads.append(
-            pltpu.make_async_copy(gate_hbm.at[0, at], gate_w.at[at], load_sem.at[0, c])
-        )
-        up_loads.append(pltpu.make_async_copy(up_hbm.at[0, at], up_w.at[at], load_sem.at[1, c]))
         down_loads.append(
             pltpu.make_async_copy(down_hbm.at[0, :, at], down_w.at[c], load_sem.at[2, c])
         )
-    for c in range(chunks):
-        gate_loads[c].start()
-        up_loads[c].start()
+    for m in range(chunks // merge):
+        gate_loads[m].start()
+        up_loads[m].start()
     for c in range(chunks):
         down_loads[c].start()
 
@@ -318,40 +325,45 @@
         pick[...] = hit.astype(bf16)
         spread[...] = jnp.transpose(jnp.where(hit, weight[0:1, :], 0.0)).astype(bf16)
 
-    def expert_in(c):
-        g = gathered[c][...] if c else gathered[c][:, :, :, :, :, ROUTE_LANES:]
-        rows_in = jnp.dot(
-            pick[...], g.reshape(tokens, cw), preferred_element_type=f32
-        ).astype(bf16)
-        gate_loads[c].wait()
-        up_loads[c].wait()
-        at = slice(c * cw, (c + 1) * cw)
+    def expert_in(m):
+        picked = []
+        for c in range(m * merge, (m + 1) * merge):
+            g = gathered[c][...] if c else gathered[c][:, :, :, :, :, ROUTE_LANES:]
+            picked.append(
+                jnp.dot(pick[...], g.reshape(tokens, cw), preferred_element_type=f32).astype(bf16)
+            )
+        rows_in = picked[0] if merge == 1 else jnp.concatenate(picked, axis=1)
+        gate_loads[m].wait()
+        up_loads[m].wait()
+        at = slice(m * merge * cw, (m + 1) * merge * cw)
         for acc, w in ((gate_acc, gate_w), (up_acc, up_w)):
             got = jnp.dot(rows_in, w[at, :], preferred_element_type=f32)
-            if c == 0:
+            if m == 0:
                 acc[...] = got
             else:
                 acc[...] += got
 
     for c in range(chunks):
         gather_z(c)
-    for s in range(chunks + 3):
+    for s in range(chunks + 5):
         if s < chunks:
             gather_z_wait(s)
             gather_push(s, 0)
         for phase in range(2):
-            c = s - 1 - phase
+            c = s - 2 - 2 * phase
             if 0 <= c < chunks:
                 gather_wait(c, phase)
                 gather_push(c, phase + 1)
-        if tasks:
-            tasks.pop(0)()
-        c = s - 3
+        for _ in range(2 if s < 4 else 1):
+            if tasks:
+                tasks.pop(0)()
+        c = s - 5
         if 0 <= c < chunks:
             gather_wait(c, 2)
             if c == 0:
                 route()
-            expert_in(c)
+            if c % merge == merge - 1:
+                expert_in(c // merge)
     for task in tasks:
         task()
 
@@ -423,14 +435,25 @@
         moe_ref[:, c * cw : (c + 1) * cw] = total.astype(bf16)
 
     stages = [stage_zero, stage_one, stage_two, stage_three, stage_four]
-    for s in range(chunks + len(stages) - 1):
-        for k, stage in enumerate(stages):
-            c = s - k
+    for s in range(chunks + OUT_LAGS[-1]):
+        for lag, stage in zip(OUT_LAGS, stages):
+            c = s - lag
             if 0 <= c < chunks:
                 stage(c)
 
     for copy in sends:
         copy.wait_send()
+
+
+def hand_on(moe_from, attn_from, moe_to, attn_to, sem):
+    copies = [
+        pltpu.make_async_copy(moe_from, moe_to, sem.at[0]),
+        pltpu.make_async_copy(attn_from, attn_to, sem.at[1]),
+    ]
+    for copy in copies:
+        copy.start()
+    for copy in copies:
+        copy.wait()
 
 
 def local_fused(
@@ -454,7 +477,7 @@
     cache, kv = cache_latent.shape[1:]
     heads = queries.shape[1]
     tokens = experts * rows
-    chunks = 7
+    chunks = CHUNKS
     cw = width // chunks
     bf16, f32 = jnp.bfloat16, jnp.float32
 
@@ -513,7 +536,7 @@
             pltpu.SemaphoreType.DMA((chunks, nz + 2)),
         ],
         compiler_params=pltpu.CompilerParams(
-            collective_id=0, has_side_effects=True, vmem_limit_bytes=60 * 1024 * 1024
+            collective_id=0, has_side_effects=True, vmem_limit_bytes=VMEM_BYTES
         ),
         name="fused_moe_attention",
     )(
@@ -528,7 +551,18 @@
         cache_latent,
         cache_rope,
     )
-    return moe_out, attn_out
+    return pl.pallas_call(
+        hand_on,
+        out_shape=(
+            jax.ShapeDtypeStruct(moe_out.shape, bf16),
+            jax.ShapeDtypeStruct(attn_out.shape, bf16),
+        ),
+        in_specs=[pl.BlockSpec(memory_space=pltpu.HBM)] * 2,
+        out_specs=(pl.BlockSpec(memory_space=pltpu.HBM),) * 2,
+        scratch_shapes=[pltpu.SemaphoreType.DMA((2,))],
+        compiler_params=pltpu.CompilerParams(vmem_limit_bytes=VMEM_BYTES),
+        name="hand_on",
+    )(moe_out, attn_out)
 
 
 def solution(mesh):

time: 79.9 us -> 74.6 us (0.934)
  local copies, waits for them, and re-layouts: 3.12 us -> 0 us
  Pallas kernels: 75.3 us -> 73.2 us
    pallas_call x1, Pallas kernels: 75.3 us -> 64.6 us  [local_fused(): pl.pallas_call(functools.partial(fused_kernel, dims, capacity), out_shape...]
    pallas_call x0 -> x1, Pallas kernels: none -> 8.57 us  [local_fused(): pl.pallas_call(hand_on, out_shape=(jax.ShapeDtypeStruct(moe_out.shape, bf...]
    unnamed x2 -> x0, local copies, waits for them, and re-layouts: 3.12 us -> none
where the time goes in v2:
time: 74.6 us; the launch traced here: 74.5 us
  Pallas kernels  73.2 us (98%)
  between operations  1.29 us (2%)
    pallas_call x1, Pallas kernels, local_fused(): pl.pallas_call(functools.partial(fused_kernel, dims, capacity), out_shape...  64.6 us
    pallas_call x1, Pallas kernels, local_fused(): pl.pallas_call(hand_on, out_shape=(jax.ShapeDtypeStruct(moe_out.shape, bf...  8.57 us

profile of v2, /device:TPU:0, one launch (start us, length us, event | category | flops | bytes accessed | tf_op | source)
XLA Modules:
  0.0 74.5 jit_solution(18161207822046359104)
XLA Ops:
  1.3 64.6 %fused_moe_attention.1 = (bf16[16,3584]{1,0:T(8,128)(2,1)}, bf16[1,128,512]{2,1,0:T(8,128)(2,1)}) custom-call(bf16[16,3584]{1,0:T(8,128)(2,1)} %x_ref.1, s32[8,16]{1,0:T(8,128)} %bitcast.4, f32[8,16]{1,0:T(8,128)} %bitcast.5, s32[1]{0:T(128)S(6)} %copy.12.len_ref, bf16[1,576,128]{2,1,0:T(8,128)(2,1)} %bitcast.3, bf16[1,3584,1024]{2,1,0:T(8,128)(2,1)} %gate_hbm.1, ...), custom_call_target="tpu_custom_call" | custom-call | tf_op jit(solution)/shard_map/fused_moe_attention/pallas_call | solution.py:491
  65.9 8.6 %hand_on.1 = (bf16[16,3584]{1,0:T(8,128)(2,1)}, bf16[1,128,512]{2,1,0:T(8,128)(2,1)}) custom-call(bf16[16,3584]{1,0:T(8,128)(2,1)} %get-tuple-element.4.moe_from, bf16[1,128,512]{2,1,0:T(8,128)(2,1)} %get-tuple-element.5.attn_from), custom_call_target="tpu_custom_call" | custom-call | tf_op jit(solution)/shard_map/hand_on/pallas_call | solution.py:554
